TPU v7x, 32 devices: a whole 2x2x4 slice. The times are simulated.
32 devices in a mesh: groups: 2 (over x), tensor: 16 (over z, y, core).
Axes of the slice: x: 2, y: 2, z: 4, core: 2. Of those that a mesh axis runs over, the one named last changes fastest.
Arguments:
- queries: bfloat16 [1024, 2048], P('groups', 'tensor'), parts along dimension 0, may hold values from -600 to 600
- block_key_rows: bfloat16 [1024, 2048], P('groups', 'tensor'), parts along dimension 0, may hold values from -5 to 5
- block_value_rows: bfloat16 [1024, 2048], P('groups', 'tensor'), parts along dimension 0, may hold values from -6 to 6
- cached_key_rows: bfloat16 [24576, 2048], P('groups', 'tensor'), parts along dimension 0, may hold values from -6 to 6
- cached_value_rows: bfloat16 [24576, 2048], P('groups', 'tensor'), parts along dimension 0, may hold values from -6 to 6
- output_projection_weight: bfloat16 [2048, 5120], P('tensor'), may hold values from -0.125 to 0.125
- stored_shrink_matrices: bfloat16 [32, 2048, 64], P('tensor'), may hold values from -0.125 to 0.125
- stored_expand_matrices: bfloat16 [32, 64, 5120], P('tensor'), may hold values from -0.75 to 0.75
- request_adapter_index: int32 [16], P('groups'), parts along dimension 0, may hold values from 0 to 31
- adapter_storage_row: int32 [32], replicated, may hold values from 0 to 31, each once
- block_token_lengths: int32 [16], P('groups'), parts along dimension 0, may hold values from 1 to 256, 512 in all
- cached_token_lengths: int32 [16], P('groups'), parts along dimension 0, may hold values from 1 to 6144, 12288 in all
Outputs:
- mixed: bfloat16 [1024, 5120], P(('groups', 'tensor')), parts along dimension 0
There are 2 independent parts, one for each index of `groups`. A program takes and returns all parts, laid end to end along the dimension named above; an argument that names none is the same for every part. Nothing has to cross between parts.
Inputs may be any that keep to these rules, and one draw needn't show every extreme that they name: `adapter_storage_row`: each adapter's row in stored_shrink_matrices and stored_expand_matrices; every row once. `block_token_lengths`: sum to 512. `cached_token_lengths`: sum to 12288.
All inputs are finite; a program needn't handle non-finite values.
Results may differ from a plain program's by a relative error of at most 0.0058.
Values may be sent and summed in bfloat16 or wider, within the bound.
A program may use at most 128 MiB of HBM per device.

v0:
```python
import jax
import jax.numpy as jnp
from jax import lax
from jax.sharding import PartitionSpec as P

HD = 128


def request_ids(lengths, total):
    segment_ends = jnp.cumsum(lengths)
    positions = jnp.arange(total, dtype=jnp.int32)
    return jnp.sum((positions[:, None] >= segment_ends[None, :]).astype(jnp.int32), axis=1)


def on_device(
    queries,
    block_key_rows,
    block_value_rows,
    cached_key_rows,
    cached_value_rows,
    output_projection_weight,
    stored_shrink_matrices,
    stored_expand_matrices,
    request_adapter_index,
    adapter_storage_row,
    block_token_lengths,
    cached_token_lengths,
):
    tensor_group_size = lax.axis_size("tensor")
    own_index = lax.axis_index("tensor")
    token_total = queries.shape[0]
    per_head_width = queries.shape[1]
    local_heads = per_head_width // HD
    cache_count = cached_key_rows.shape[0]
    request_total = block_token_lengths.shape[0]
    adapter_rank_size = stored_shrink_matrices.shape[2]
    rank_portion = adapter_rank_size // tensor_group_size
    model_width = output_projection_weight.shape[1]
    adapter_row_ids = adapter_storage_row[request_adapter_index]
    adapters_a, adapters_b = (
        lax.all_to_all(stored_shrink_matrices, "tensor", split_axis=1, concat_axis=0, tiled=True),
        lax.all_to_all(stored_expand_matrices, "tensor", split_axis=1, concat_axis=0, tiled=True),
    )
    shrink_matrix_list = adapters_a[adapter_row_ids]
    expand_matrix_list = adapters_b[adapter_row_ids]
    token_req = request_ids(block_token_lengths, token_total)
    cache_req = request_ids(cached_token_lengths, cache_count)
    key_req = jnp.concatenate([cache_req, token_req])
    token_pos = jnp.arange(token_total, dtype=jnp.int32)
    key_pos = jnp.concatenate([jnp.full((cache_count,), -1, jnp.int32), token_pos])
    visible = (key_req[None, :] == token_req[:, None]) & (key_pos[None, :] <= token_pos[:, None])
    all_keys = jnp.concatenate([cached_key_rows, block_key_rows], axis=0)
    all_values = jnp.concatenate([cached_value_rows, block_value_rows], axis=0)
    key_total = all_keys.shape[0]
    query_heads = queries.reshape(token_total, local_heads, HD)
    key_heads = all_keys.reshape(key_total, local_heads, HD)
    value_heads = all_values.reshape(key_total, local_heads, HD)
    score_scale = HD ** (-0.5)
    scores = (
        jnp.einsum("qhd,khd->hqk", query_heads, key_heads, preferred_element_type=jnp.float32)
        * score_scale
    )
    scores = jnp.where(visible[None, :, :], scores, -jnp.inf)
    weights = jax.nn.softmax(scores, axis=2).astype(jnp.bfloat16)
    attended = jnp.einsum("hqk,khd->qhd", weights, value_heads, preferred_element_type=jnp.float32)
    attended = attended.astype(jnp.bfloat16).reshape(token_total, per_head_width)
    shrink_flattened = shrink_matrix_list.transpose(1, 0, 2).reshape(
        per_head_width, request_total * adapter_rank_size
    )
    shrink_every_token = jnp.dot(attended, shrink_flattened, preferred_element_type=jnp.float32)
    shrink_every_token = shrink_every_token.reshape(token_total, request_total, adapter_rank_size)
    onehot = (token_req[:, None] == jnp.arange(request_total, dtype=jnp.int32)[None, :]).astype(
        jnp.float32
    )
    partial_shrunk = jnp.sum(shrink_every_token * onehot[:, :, None], axis=1)
    shrunk = lax.psum(partial_shrunk, "tensor")
    own_ranks = lax.dynamic_slice_in_dim(shrunk, own_index * rank_portion, rank_portion, 1)
    expanded = (onehot[:, :, None] * own_ranks[:, None, :]).reshape(
        token_total, request_total * rank_portion
    )
    expand_rows = expand_matrix_list.reshape(request_total * rank_portion, model_width).astype(
        jnp.float32
    )
    base_part = jnp.dot(attended, output_projection_weight, preferred_element_type=jnp.float32)
    summed = lax.psum_scatter(
        base_part + jnp.dot(expanded, expand_rows, precision=lax.Precision.HIGHEST),
        "tensor",
        scatter_dimension=0,
        tiled=True,
    )
    return summed.astype(jnp.bfloat16)


def solution(mesh):
    placed = (
        P("groups", "tensor"),
        P("groups", "tensor"),
        P("groups", "tensor"),
        P("groups", "tensor"),
        P("groups", "tensor"),
        P("tensor", None),
        P("tensor", None, None),
        P("tensor", None, None),
        P("groups"),
        P(),
        P("groups"),
        P("groups"),
    )
    return jax.shard_map(
        on_device,
        mesh=mesh,
        in_specs=placed,
        out_specs=P(("groups", "tensor"), None),
        check_vma=False,
    )
```

profile of v0, /device:TPU:27, one launch (start us, length us, event | category | flops | bytes accessed | tf_op | source)
XLA Modules:
  0.0 307.6 jit_solution(5115299236932868234)
XLA Ops:
  6.5 0.0 copy-start
  6.5 0.0 copy-start.4
  6.5 0.0 copy-start.2
  6.5 0.0 copy-start.3
  6.5 2.5 copy.28
  9.0 1.5 reshape.158
  10.5 6.4 %all-to-all-start = ((bf16[16,2,8192]{2,1,0:T(2,128)(2,1)}), bf16[16,2,8192]{2,1,0:T(2,128)(2,1)S(1)}, u32[]{:S(2)}, u32[]{:S(2)}) async-start(bf16[16,2,8192]{2,1,0:T(2,128)(2,1)} %reshape.158), calls=%async_computation | async-start | bytes 1048576 | tf_op jit(solution)/shard_map/all_to_all | solution.py:41
  16.9 0.8 reduce-window.17
  17.7 0.1 convert_reduce_fusion.1
  17.8 0.8 reduce-window.16
  18.7 0.2 convert_reduce_fusion
  18.9 0.7 compare_select_fusion.1
  19.6 1.3 gather_fusion
  20.9 3.7 %copy.32 = bf16[2,64,5120]{2,0,1:T(2,128)(2,1)} copy(bf16[2,64,5120]{2,1,0:T(8,128)(2,1)} %param.19) | data formatting | bytes 2621440 | tf_op args[7]
  24.6 0.0 copy-done.4
  24.6 0.0 copy-done.2
  24.6 0.0 copy-done.3
  24.6 15.8 %fusion.25 = (f32[512]{0:T(512)S(1)}, f32[512,12800]{0,1:T(8,128)S(1)}) fusion(bf16[512,128]{1,0:T(8,128)(2,1)S(1)} %copy-done.2, bf16[512,128]{1,0:T(8,128)(2,1)S(1)} %copy-done.3, bf16[12288,128]{1,0:T(8,128)(2,1)} %param.15, s32[12800]{0:T(1024)S(1)} %copy-done.4, s32[512]{0:T(512)S(1)} %convert_reduce_fusion.1, s32[12800]{0:T(1024)S(1)} %pad_add_fusion), kind=kOutput, calls=%fused_computation.43 | convolution fusion | flops 1723596288 | bytes 29728768 | tf_op jit(solution)/shard_map/qhd,khd->hqk/dot_general | solution.py:60
  40.4 0.0 copy-start.1
  40.4 8.6 %copy-done.1 = f32[512,12800]{0,1:T(8,128)} copy-done((f32[512,12800]{0,1:T(8,128)}, f32[512,12800]{0,1:T(8,128)S(1)}, u32[]{:S(2)}) %copy-start.1) | copy-done | bytes 26214424
  49.1 3.9 %fusion.1 = f32[512]{0:T(512)S(1)} fusion(f32[512,12800]{0,1:T(8,128)S(1)} %get-tuple-element.6, f32[512]{0:T(512)S(1)} %get-tuple-element.5), kind=kLoop, calls=%fused_computation.8 | loop fusion | flops 13106688 | bytes 26218496 | tf_op jit(solution)/shard_map/reduce_sum | solution.py:64
  53.0 0.0 all-to-all-done
  53.0 6.0 %all-to-all-start.1 = ((bf16[2,64,5120]{2,0,1:T(2,128)(2,1)}), bf16[2,64,5120]{2,0,1:T(2,128)(2,1)S(1)}, u32[]{:S(2)}, u32[]{:S(2)}) async-start(bf16[2,64,5120]{2,0,1:T(2,128)(2,1)} %copy.32), calls=%async_computation.1 | async-start | bytes 2621440 | tf_op jit(solution)/shard_map/all_to_all | solution.py:42
  59.0 0.0 all-reduce.2.cloned.1.call-start
  59.0 12.0 %fusion.10 = bf16[128,512]{1,0:T(8,128)(2,1)S(1)} fusion(f32[512,12800]{0,1:T(8,128)} %copy-done.1, f32[512]{0:T(512)S(1)} %fusion.1, f32[512]{0:T(512)S(1)} %get-tuple-element.5, bf16[512,128]{1,0:T(8,128)(2,1)} %param.14, bf16[12288,128]{1,0:T(8,128)(2,1)} %param.16), kind=kOutput, calls=%fused_computation.19 | convolution fusion | flops 1704001536 | bytes 29626368 | tf_op jit(solution)/shard_map/hqk,khd->qhd/dot_general | solution.py:65
  71.0 1.7 reshape.159
  72.7 2.4 copy.38
  75.1 0.6 gather_fusion.1
  75.6 0.9 fusion.9
  76.6 0.0 all-reduce.2.cloned.1.call-update
  76.6 0.2 reduce-scatter.2.cloned.1.call-start
  76.8 86.4 %all-reduce.2.cloned.1.call-done = f32[512,64]{0,1:T(8,128)} async-done(((f32[512,64]{0,1:T(8,128)}), f32[512,64]{0,1:T(8,128)}) %all-reduce.2.cloned.1.call-update) | async-done | bytes 131088 | tf_op jit(solution)/shard_map/psum | solution.py:76
  163.2 0.7 constant_dynamic-slice_fusion
  164.0 0.0 all-to-all-done.1
  164.0 1.7 copy.33
  165.6 2.1 gather_fusion.2
  167.8 4.3 %fusion.13 = f32[512,5120,1]{1,0,2:T(8,128)S(1)} fusion(bf16[8,4,5120]{2,1,0:T(4,128)(2,1)S(1)} %gather_fusion.2, f32[512,4]{0,1:T(4,128)S(1)} %constant_dynamic-slice_fusion, f32[512,8]{0,1:T(8,128)S(1)} %fusion.21), kind=kOutput, calls=%fused_computation.22 | convolution fusion | flops 1006649344 | bytes 10838016 | tf_op jit(solution)/shard_map/dot_general | solution.py:86
  172.1 0.0 copy-done
  172.1 5.6 %bitcast_add_fusion = f32[512,5120]{1,0:T(8,128)} fusion(f32[512,5120,1]{1,0,2:T(8,128)S(1)} %fusion.13, bf16[128,5120]{1,0:T(8,128)(2,1)S(1)} %copy-done, bf16[128,512]{1,0:T(8,128)(2,1)S(1)} %fusion.10), kind=kOutput, calls=%fused_computation.10 | convolution fusion | flops 673710080 | bytes 22413312 | tf_op jit(solution)/shard_map/dot_general | solution.py:84
  177.7 0.0 reduce-scatter.2.cloned.1.call-update
  177.7 121.3 %reduce-scatter.2.cloned.1.call-done = f32[32,5120]{1,0:T(8,128)} async-done(((f32[512,5120]{1,0:T(8,128)}), f32[32,5120]{1,0:T(8,128)}) %reduce-scatter.2.cloned.1.call-update) | async-done | bytes 655376 | tf_op jit(solution)/shard_map/reduce_scatter | solution.py:85
  299.0 1.8 convert_element_type.37
  (5 shorter events, 0.0 us)
Async XLA Ops:
  6.5 165.5 %copy-start = (bf16[128,5120]{1,0:T(8,128)(2,1)S(1)}, bf16[128,5120]{1,0:T(8,128)(2,1)}, u32[]{:S(2)}) copy-start(bf16[128,5120]{1,0:T(8,128)(2,1)} %param.17) | copy-start | bytes 3932164
  6.5 18.1 %copy-start.4 = (s32[12800]{0:T(1024)S(1)}, s32[12800]{0:T(1024)}, u32[]{:S(2)}) copy-start(s32[12800]{0:T(1024)} %constant.10.clone.1) | copy-start | bytes 153604
  6.5 18.1 %copy-start.2 = (bf16[512,128]{1,0:T(8,128)(2,1)S(1)}, bf16[512,128]{1,0:T(8,128)(2,1)}, u32[]{:S(2)}) copy-start(bf16[512,128]{1,0:T(8,128)(2,1)} %param.12) | copy-start | bytes 393220
  6.5 18.1 %copy-start.3 = (bf16[512,128]{1,0:T(8,128)(2,1)S(1)}, bf16[512,128]{1,0:T(8,128)(2,1)}, u32[]{:S(2)}) copy-start(bf16[512,128]{1,0:T(8,128)(2,1)} %param.13) | copy-start | bytes 393220
  10.5 42.4 %all-to-all-start = ((bf16[16,2,8192]{2,1,0:T(2,128)(2,1)}), bf16[16,2,8192]{2,1,0:T(2,128)(2,1)S(1)}, u32[]{:S(2)}, u32[]{:S(2)}) async-start(bf16[16,2,8192]{2,1,0:T(2,128)(2,1)} %reshape.158), calls=%async_computation | async-start | bytes 1048576 | tf_op jit(solution)/shard_map/all_to_all | solution.py:41
  40.4 8.6 %copy-start.1 = (f32[512,12800]{0,1:T(8,128)}, f32[512,12800]{0,1:T(8,128)S(1)}, u32[]{:S(2)}) copy-start(f32[512,12800]{0,1:T(8,128)S(1)} %get-tuple-element.6) | copy-start | bytes 78643200
  53.0 111.0 %all-to-all-start.1 = ((bf16[2,64,5120]{2,0,1:T(2,128)(2,1)}), bf16[2,64,5120]{2,0,1:T(2,128)(2,1)S(1)}, u32[]{:S(2)}, u32[]{:S(2)}) async-start(bf16[2,64,5120]{2,0,1:T(2,128)(2,1)} %copy.32), calls=%async_computation.1 | async-start | bytes 2621440 | tf_op jit(solution)/shard_map/all_to_all | solution.py:42
  59.0 104.2 %all-reduce.2.cloned.1.call-start = ((), (), s32[]{:S(2)}) async-start(), calls=%async_computation.3 | async-start | bytes 262144 | tf_op jit(solution)/shard_map/psum | solution.py:76
  76.6 222.4 %reduce-scatter.2.cloned.1.call-start = ((), (), s32[]{:S(2)}) async-start(), calls=%async_computation.4 | async-start | bytes 11141120 | tf_op jit(solution)/shard_map/reduce_scatter | solution.py:85
Sparse Core Ops, SparseCore 0:
  76.7 86.4 all-reduce.1
  177.8 121.1 reduce-scatter.1
where the time goes:
time: 311 us; the launch traced here: 308 us
  waiting for transfers between devices  208 us (67%)
  matrix products  38.6 us (12%)
  local copies, waits for them, and re-layouts  26.7 us (9%)
  between operations  13.5 us (4%)
  starting transfers between devices  12.7 us (4%)
  other arithmetic  8.43 us (3%)
    reduce_scatter x1, waiting for transfers between devices, on_device(): lax.psum_scatter(base_part + jnp.dot(expanded, expand_rows, precision=lax...  121 us
    psum x1, waiting for transfers between devices, on_device(): shrunk = lax.psum(partial_shrunk, 'tensor')  86.4 us
    unnamed x14, local copies, waits for them, and re-layouts  18 us
    dot_general x1, matrix products, on_device(): jnp.einsum('qhd,khd->hqk', query_heads, key_heads, preferred_element_type...  15.8 us
    dot_general x1, matrix products, on_device(): jnp.einsum('hqk,khd->qhd', weights, value_heads, preferred_element_type=j...  12 us
    all_to_all x1, starting transfers between devices, on_device(): lax.all_to_all(stored_shrink_matrices, 'tensor', split_axis=1, concat_axi...  6.39 us
  transfers between devices with their start and end apart: 4, of which 2 were waited for; matrix products, arithmetic and copies ran while one was open for 15% of the time, Pallas kernels for 0%

commit v1 on v0

v1 whole, which is shorter than its diff:
```python
import functools
import math

import jax
import jax.numpy as jnp
from jax import lax
from jax.experimental import pallas as pl
from jax.experimental.pallas import tpu as pltpu
from jax.sharding import PartitionSpec as P

HD = 128
SUB = 4
BIG = 2.0**40
F32 = jnp.float32
BF16 = jnp.bfloat16


def dot_nt(a, b):
    return lax.dot_general(a, b, (((1,), (1,)), ((), ())), preferred_element_type=F32)


def pick(position, bounds, values, like):
    out = like
    for r, value in enumerate(values):
        inside = (position >= bounds[r]) & (position < bounds[r + 1])
        out = jnp.where(inside, value, out)
    return out


def kernel(
    n,
    q_chunk,
    key_block,
    q_hbm,
    bk_hbm,
    bv_hbm,
    ck_hbm,
    cv_hbm,
    w_hbm,
    s_hbm,
    e_hbm,
    req_adapter,
    storage_row,
    block_len,
    cache_len,
    out_ref,
    q2,
    k2,
    v2,
    w_all,
    e_all,
    s_all,
    att_all,
    shr_part,
    shr_recv,
    shr_full,
    part,
    recv,
    base,
    load_sem,
    w_send,
    w_recv,
    e_send,
    e_recv,
    s_send,
    s_recv,
    a_send,
    a_recv,
    p_send,
    p_recv,
    f_send,
    f_recv,
    o_send,
    o_recv,
):
    t = lax.axis_index("tensor")
    j = lax.rem(t, SUB)
    first = t - j
    tokens = q_hbm.shape[0]
    cached = ck_hbm.shape[0]
    requests = block_len.shape[0]
    rows = tokens // n
    width = w_hbm.shape[1] // SUB
    own_adapters = s_hbm.shape[0]
    chunks = tokens // q_chunk
    per_chunk = n // chunks

    loads = [
        pltpu.make_async_copy(q_hbm, q2.at[:, pl.ds(0, HD)], load_sem.at[0]),
        pltpu.make_async_copy(bk_hbm, k2.at[pl.ds(0, tokens), pl.ds(0, HD)], load_sem.at[1]),
        pltpu.make_async_copy(ck_hbm, k2.at[pl.ds(tokens, cached), pl.ds(0, HD)], load_sem.at[2]),
        pltpu.make_async_copy(bv_hbm, v2.at[pl.ds(0, tokens), pl.ds(0, HD)], load_sem.at[3]),
        pltpu.make_async_copy(cv_hbm, v2.at[pl.ds(tokens, cached), pl.ds(0, HD)], load_sem.at[4]),
    ]
    for load in loads:
        load.start()

    def columns(block):
        return pl.ds(pl.multiple_of(block * width, 128), width)

    def heads_columns(device):
        return pl.ds(pl.multiple_of(device * HD, HD), HD)

    own_loads = [
        pltpu.make_async_copy(w_hbm.at[:, columns(j)], w_all.at[j], load_sem.at[5]),
        pltpu.make_async_copy(e_hbm.at[:, columns(j)], e_all.at[j], load_sem.at[6]),
        pltpu.make_async_copy(s_hbm.at[:, :, heads_columns(t)], s_all.at[t], load_sem.at[7]),
    ]
    for load in own_loads:
        load.start()

    barrier = pltpu.get_barrier_semaphore()
    for k in range(1, n):
        pl.semaphore_signal(
            barrier,
            inc=1,
            device_id={"tensor": lax.rem(t + k, n)},
            device_id_type=pl.DeviceIdType.MESH,
        )
    pl.semaphore_wait(barrier, n - 1)

    def remote(src, dst, send_sem, recv_sem, device):
        return pltpu.make_async_remote_copy(
            src_ref=src,
            dst_ref=dst,
            send_sem=send_sem,
            recv_sem=recv_sem,
            device_id={"tensor": device},
            device_id_type=pl.DeviceIdType.MESH,
        )

    def shrink_copy(k, sender, device):
        return remote(
            s_hbm.at[:, :, heads_columns(device)], s_all.at[sender], s_send.at[k], s_recv.at[k], device
        )

    def weight_copy(k, sender_j, jj):
        return remote(
            w_hbm.at[:, columns(jj)], w_all.at[sender_j], w_send.at[k], w_recv.at[k], first + jj
        )

    def expand_copy(k, sender_j, jj):
        return remote(
            e_hbm.at[:, columns(jj)], e_all.at[sender_j], e_send.at[k], e_recv.at[k], first + jj
        )

    for k in range(1, n):
        shrink_copy(k, t, lax.rem(t + k, n)).start()
    for k in range(1, SUB):
        weight_copy(k, j, lax.rem(j + k, SUB)).start()
    for k in range(1, SUB):
        expand_copy(k, j, lax.rem(j + k, SUB)).start()

    token_bounds, cache_bounds, adapter_rows = [jnp.int32(0)], [jnp.int32(0)], []
    for r in range(requests):
        token_bounds.append(token_bounds[r] + block_len[r])
        cache_bounds.append(cache_bounds[r] + cache_len[r])
        adapter_rows.append(storage_row[req_adapter[r]])

    lane1 = lax.broadcasted_iota(jnp.int32, (1, HD), 1)
    token_lo = jnp.zeros((1, HD), jnp.int32)
    token_hi = jnp.zeros((1, HD), jnp.int32)
    cache_lo = jnp.zeros((1, HD), jnp.int32)
    cache_hi = jnp.zeros((1, HD), jnp.int32)
    for r in range(requests):
        token_lo = jnp.where(lane1 == r, token_bounds[r], token_lo)
        token_hi = jnp.where(lane1 == r, token_bounds[r + 1], token_hi)
        cache_lo = jnp.where(lane1 == r, cache_bounds[r], cache_lo)
        cache_hi = jnp.where(lane1 == r, cache_bounds[r + 1], cache_hi)
    token_pos = lax.broadcasted_iota(jnp.int32, (tokens, HD), 0)
    token_in = (token_pos >= token_lo) & (token_pos < token_hi)
    q2[:, HD:] = jnp.where(token_in, 0.0, -BIG).astype(BF16)
    k2[0:tokens, HD:] = jnp.where(token_in, 1.0, 0.0).astype(BF16)
    ones = jnp.ones((tokens, HD), BF16)
    v2[0:tokens, HD:] = ones

    def augment(i, carry):
        at = pl.multiple_of(tokens + i * tokens, tokens)
        pos = token_pos + i * tokens
        inside = (pos >= cache_lo) & (pos < cache_hi)
        k2[pl.ds(at, tokens), HD:] = jnp.where(inside, 1.0, 0.0).astype(BF16)
        v2[pl.ds(at, tokens), HD:] = ones
        return carry

    lax.fori_loop(0, cached // tokens, augment, 0)
    for load in loads:
        load.wait()
    for load in own_loads:
        load.wait()

    scale = HD**-0.5 * math.log2(math.e)
    adapters = n * own_adapters

    def att_copy(c, k, sender_j, jj):
        span = pl.ds(c * q_chunk, q_chunk)
        return remote(
            att_all.at[sender_j, span],
            att_all.at[sender_j, span],
            a_send.at[c, k],
            a_recv.at[c, k],
            first + jj,
        )

    def row_slice(ref, device):
        return ref.at[pl.ds(pl.multiple_of(device * rows, rows), rows)]

    def shr_copy(sender, device):
        return remote(
            row_slice(shr_part, device),
            shr_recv.at[sender],
            p_send.at[device],
            p_recv.at[sender],
            device,
        )

    for c in range(chunks):
        q = q2[pl.ds(c * q_chunk, q_chunk), :]
        scores = dot_nt(q, k2[0:tokens, :])
        row = lax.broadcasted_iota(jnp.int32, scores.shape, 0) + c * q_chunk
        col = lax.broadcasted_iota(jnp.int32, scores.shape, 1)
        scores = jnp.where(col <= row, scores, -BIG)
        top = jnp.max(scores, axis=1, keepdims=True)
        p = jnp.exp2((scores - top) * scale).astype(BF16)
        acc = jnp.dot(p, v2[0:tokens, :], preferred_element_type=F32)

        def step(i, carry):
            top, acc = carry
            at = pl.multiple_of(tokens + i * key_block, 512)
            scores = dot_nt(q, k2[pl.ds(at, key_block), :])
            new_top = jnp.maximum(top, jnp.max(scores, axis=1, keepdims=True))
            p = jnp.exp2((scores - new_top) * scale).astype(BF16)
            acc = acc * jnp.exp2((top - new_top) * scale)
            return new_top, acc + jnp.dot(p, v2[pl.ds(at, key_block), :], preferred_element_type=F32)

        top, acc = lax.fori_loop(0, cached // key_block, step, (top, acc))
        attended = (acc[:, :HD] / acc[:, HD:]).astype(BF16)
        span = pl.ds(c * q_chunk, q_chunk)
        att_all[j, span] = attended
        for k in range(1, SUB):
            att_copy(c, k, j, lax.rem(j + k, SUB)).start()

        if c == 0:
            for k in range(1, n):
                shrink_copy(k, lax.rem(t + n - k, n), t).wait_recv()
        pos = lax.broadcasted_iota(jnp.int32, (q_chunk, HD), 0) + c * q_chunk
        lane = lax.broadcasted_iota(jnp.int32, (q_chunk, HD), 1)
        token_row = pick(pos, token_bounds, adapter_rows, jnp.zeros((q_chunk, HD), jnp.int32))
        half = jnp.where(lane >= HD // 2, 1, 0)
        shr = jnp.zeros((q_chunk, HD), F32)
        for a in range(0, adapters, 2):
            matrices = s_all[a // own_adapters].reshape(HD, HD)
            product = dot_nt(attended, matrices)
            shr = jnp.where(token_row == half + a, product, shr)
        shr_part[span, :] = shr + pltpu.roll(shr, HD // 2, 1)
        for k in range(per_chunk):
            device = c * per_chunk + lax.rem(t + k, per_chunk)

            @pl.when(device != t)
            def _():
                shr_copy(t, device).start()

    total = row_slice(shr_part, t)[...]
    for k in range(1, n):
        sender = lax.rem(t + n - k, n)
        shr_copy_in = remote(
            row_slice(shr_part, t), shr_recv.at[sender], p_send.at[sender], p_recv.at[sender], sender
        )
        shr_copy_in.wait_recv()
        total = total + shr_recv[sender]
    row_slice(shr_full, t)[...] = total

    def full_copy(k, sender, device):
        return remote(
            row_slice(shr_full, sender), row_slice(shr_full, sender), f_send.at[k], f_recv.at[k], device
        )

    for k in range(1, n):
        full_copy(k, t, lax.rem(t + k, n)).start()

    for k in range(1, SUB):
        source = lax.rem(j + SUB - k, SUB)
        weight_copy(k, source, j).wait_recv()
        for c in range(chunks):
            att_copy(c, k, source, j).wait_recv()
    for c in range(chunks):
        span = pl.ds(c * q_chunk, q_chunk)
        value = jnp.dot(att_all[0, span], w_all[0], preferred_element_type=F32)
        for s in range(1, SUB):
            value = value + jnp.dot(att_all[s, span], w_all[s], preferred_element_type=F32)
        base[span, :] = value

    for k in range(1, SUB):
        expand_copy(k, lax.rem(j + SUB - k, SUB), j).wait_recv()
    for k in range(1, n):
        full_copy(k, lax.rem(t + n - k, n), t).wait_recv()

    def part_copy(sender, device):
        return remote(part.at[device], recv.at[sender], o_send.at[device], o_recv.at[sender], device)

    for c in range(chunks):
        span = pl.ds(c * q_chunk, q_chunk)
        pos = lax.broadcasted_iota(jnp.int32, (q_chunk, HD), 0) + c * q_chunk
        lane = lax.broadcasted_iota(jnp.int32, (q_chunk, HD), 1)
        token_row = pick(pos, token_bounds, adapter_rows, jnp.zeros((q_chunk, HD), jnp.int32))
        half = jnp.where(lane >= HD // 2, 1, 0)
        shrunk = shr_full[span, :]
        value = base[span, :]
        for s in range(SUB):
            mine = jnp.where(token_row == half + (first + s) * own_adapters, shrunk, 0.0)
            high = mine.astype(BF16)
            low = (mine - high.astype(F32)).astype(BF16)
            value = value + jnp.dot(high, e_all[s], preferred_element_type=F32)
            value = value + jnp.dot(low, e_all[s], preferred_element_type=F32)
        per = value.astype(part.dtype).reshape(per_chunk, rows, width)
        part[pl.ds(c * per_chunk, per_chunk)] = per
        for k in range(per_chunk):
            device = c * per_chunk + lax.rem(t + k, per_chunk)

            @pl.when(device != t)
            def _():
                part_copy(t, device).start()

    recv[t] = part[t]
    for k in range(1, n):
        sender = lax.rem(t + n - k, n)
        part_in = remote(part.at[sender], recv.at[sender], o_send.at[sender], o_recv.at[sender], sender)
        part_in.wait_recv()
    for s in range(SUB):
        value = recv[s].astype(F32)
        for z in range(1, n // SUB):
            value = value + recv[z * SUB + s].astype(F32)
        out_ref[:, s * width : (s + 1) * width] = value.astype(out_ref.dtype)

    for k in range(1, n):
        device = lax.rem(t + k, n)
        shrink_copy(k, t, device).wait_send()
        full_copy(k, t, device).wait_send()
        shr_copy(t, device).wait_send()
        part_copy(t, device).wait_send()
    for k in range(1, SUB):
        jj = lax.rem(j + k, SUB)
        weight_copy(k, j, jj).wait_send()
        expand_copy(k, j, jj).wait_send()
        for c in range(chunks):
            att_copy(c, k, j, jj).wait_send()


def on_device(
    queries,
    block_key_rows,
    block_value_rows,
    cached_key_rows,
    cached_value_rows,
    output_projection_weight,
    stored_shrink_matrices,
    stored_expand_matrices,
    request_adapter_index,
    adapter_storage_row,
    block_token_lengths,
    cached_token_lengths,
):
    n = lax.axis_size("tensor")
    tokens = queries.shape[0]
    cached = cached_key_rows.shape[0]
    model = output_projection_weight.shape[1]
    own, _, rank = stored_shrink_matrices.shape
    rows = tokens // n
    width = model // SUB
    q_chunk = 256
    key_block = 1536
    chunks = tokens // q_chunk
    send_type = BF16 if rows % 16 == 0 else F32
    shrink_t = stored_shrink_matrices.transpose(0, 2, 1)
    expand = stored_expand_matrices.reshape(own * rank, model)
    hbm = pl.BlockSpec(memory_space=pl.ANY)
    smem = pl.BlockSpec(memory_space=pltpu.SMEM)
    dma = pltpu.SemaphoreType.DMA
    return pl.pallas_call(
        functools.partial(kernel, n, q_chunk, key_block),
        out_shape=jax.ShapeDtypeStruct((rows, model), BF16),
        in_specs=[hbm] * 8 + [smem] * 4,
        out_specs=pl.BlockSpec(memory_space=pltpu.VMEM),
        scratch_shapes=[
            pltpu.VMEM((tokens, 2 * HD), BF16),
            pltpu.VMEM((tokens + cached, 2 * HD), BF16),
            pltpu.VMEM((tokens + cached, 2 * HD), BF16),
            pltpu.VMEM((SUB, HD, width), BF16),
            pltpu.VMEM((SUB, own * rank, width), BF16),
            pltpu.VMEM((n, own, rank, HD), BF16),
            pltpu.VMEM((SUB, tokens, HD), BF16),
            pltpu.VMEM((tokens, HD), F32),
            pltpu.VMEM((n, rows, HD), F32),
            pltpu.VMEM((tokens, HD), F32),
            pltpu.VMEM((n, rows, width), send_type),
            pltpu.VMEM((n, rows, width), send_type),
            pltpu.VMEM((tokens, width), F32),
            dma((8,)),
            dma((SUB,)),
            dma((SUB,)),
            dma((SUB,)),
            dma((SUB,)),
            dma((n,)),
            dma((n,)),
            dma((chunks, SUB)),
            dma((chunks, SUB)),
            dma((n,)),
            dma((n,)),
            dma((n,)),
            dma((n,)),
            dma((n,)),
            dma((n,)),
        ],
        compiler_params=pltpu.CompilerParams(
            collective_id=0, has_side_effects=True, vmem_limit_bytes=56 * 1024 * 1024
        ),
    )(
        queries,
        block_key_rows,
        block_value_rows,
        cached_key_rows,
        cached_value_rows,
        output_projection_weight,
        shrink_t,
        expand,
        request_adapter_index,
        adapter_storage_row,
        block_token_lengths,
        cached_token_lengths,
    )


def solution(mesh):
    placed = (
        P("groups", "tensor"),
        P("groups", "tensor"),
        P("groups", "tensor"),
        P("groups", "tensor"),
        P("groups", "tensor"),
        P("tensor", None),
        P("tensor", None, None),
        P("tensor", None, None),
        P("groups"),
        P(),
        P("groups"),
        P("groups"),
    )
    return jax.shard_map(
        on_device,
        mesh=mesh,
        in_specs=placed,
        out_specs=P(("groups", "tensor"), None),
        check_vma=False,
    )
```

time: 311 us -> 93.9 us (0.30); the launches traced: 308 us -> 93.7 us
  waiting for transfers between devices: 208 us -> 0 us
  Pallas kernels: 0 us -> 92 us
  matrix products: 38.6 us -> 0 us
  local copies, waits for them, and re-layouts: 26.7 us -> 1.72 us
  between operations: 13.5 us -> 0.01 us
  starting transfers between devices: 12.7 us -> 0 us
  other arithmetic: 8.43 us -> 0 us
    reduce_scatter x1 -> x0, waiting for transfers between devices: 121 us -> none  [on_device(): lax.psum_scatter(base_part + jnp.dot(expanded, expand_rows, precision=lax...]
    pallas_call x0 -> x1, Pallas kernels: none -> 92 us  [on_device(): pl.pallas_call(functools.partial(kernel, n, q_chunk, key_block), out_shap...]
    psum x1 -> x0, waiting for transfers between devices: 86.4 us -> none  [on_device(): shrunk = lax.psum(partial_shrunk, 'tensor')]
    dot_general x5 -> x0, matrix products: 38.6 us -> none  [the longest x1 15.8 us: on_device(): jnp.einsum('qhd,khd->hqk', query_heads, key_heads, preferred_element_type...]
    unnamed x14 -> x1, local copies, waits for them, and re-layouts: 18 us -> 1.72 us
    all_to_all x2 -> x0, starting transfers between devices: 12.4 us -> none  [the longest x1 6.39 us: on_device(): lax.all_to_all(stored_shrink_matrices, 'tensor', split_axis=1, concat_axi...]
    reduce_sum x3 -> x0, other arithmetic: 4.23 us -> none  [the longest x1 3.91 us: on_device(): weights = jax.nn.softmax(scores, axis=2).astype(jnp.bfloat16)]
    gather x3 -> x0, local copies, waits for them, and re-layouts: 4.01 us -> none  [the longest x1 2.14 us: on_device(): expand_matrix_list = adapters_b[adapter_row_ids]]
  transfers between devices with their start and end apart: 4 -> 0, of which waited for: 2 -> 0; matrix products, arithmetic and copies ran while one was open for 15% -> 0% of each run, Pallas kernels for 0% -> 0%
where the time goes in v1:
time: 93.9 us; the launch traced here: 93.7 us
  Pallas kernels  92 us (98%)
  local copies, waits for them, and re-layouts  1.72 us (2%)
    pallas_call x1, Pallas kernels, on_device(): pl.pallas_call(functools.partial(kernel, n, q_chunk, key_block), out_shap...  92 us

profile of v1, /device:TPU:27, one launch (start us, length us, event | category | flops | bytes accessed | tf_op | source)
XLA Modules:
  0.0 93.7 jit_solution(15122661842456981598)
XLA Ops:
  0.0 92.0 %shard_map.118 = bf16[32,5120]{1,0:T(8,128)(2,1)} custom-call(bf16[512,128]{1,0:T(8,128)(2,1)} %q_hbm.1, bf16[512,128]{1,0:T(8,128)(2,1)} %bk_hbm.1, bf16[512,128]{1,0:T(8,128)(2,1)} %bv_hbm.1, bf16[12288,128]{1,0:T(8,128)(2,1)} %ck_hbm.1, bf16[12288,128]{1,0:T(8,128)(2,1)} %cv_hbm.1, bf16[128,5120]{1,0:T(8,128)(2,1)} %w_hbm.1, ...), custom_call_target="tpu_custom_call" | custom-call | tf_op jit(solution)/shard_map/pallas_call | solution.py:378
  92.0 1.7 %copy.14 = bf16[32,5120]{1,0:T(8,128)(2,1)} copy(bf16[32,5120]{1,0:T(8,128)(2,1)} %shard_map.118) | data formatting | bytes 655360

commit v2 on v1

--- a/solution.py
+++ b/solution.py
@@ -9,7 +9,7 @@
 from jax.sharding import PartitionSpec as P
 
 HD = 128
-SUB = 4
+SUB = 8
 BIG = 2.0**40
 F32 = jnp.float32
 BF16 = jnp.bfloat16
@@ -25,6 +25,17 @@
         inside = (position >= bounds[r]) & (position < bounds[r + 1])
         out = jnp.where(inside, value, out)
     return out
+
+
+def pack(twice, kind):
+    high = twice.astype(BF16).astype(F32)
+    lane = lax.broadcasted_iota(jnp.int32, twice.shape, 1)
+    return jnp.where(lane < HD // 2, high, twice - high).astype(kind)
+
+
+def unpack(packed):
+    halves = packed.astype(F32)
+    return halves + pltpu.roll(halves, HD // 2, 1)
 
 
 def kernel(
@@ -251,7 +262,7 @@
             matrices = s_all[a // own_adapters].reshape(HD, HD)
             product = dot_nt(attended, matrices)
             shr = jnp.where(token_row == half + a, product, shr)
-        shr_part[span, :] = shr + pltpu.roll(shr, HD // 2, 1)
+        shr_part[span, :] = pack(shr + pltpu.roll(shr, HD // 2, 1), shr_part.dtype)
         for k in range(per_chunk):
             device = c * per_chunk + lax.rem(t + k, per_chunk)
 
@@ -259,15 +270,15 @@
             def _():
                 shr_copy(t, device).start()
 
-    total = row_slice(shr_part, t)[...]
+    total = unpack(row_slice(shr_part, t)[...])
     for k in range(1, n):
         sender = lax.rem(t + n - k, n)
         shr_copy_in = remote(
             row_slice(shr_part, t), shr_recv.at[sender], p_send.at[sender], p_recv.at[sender], sender
         )
         shr_copy_in.wait_recv()
-        total = total + shr_recv[sender]
-    row_slice(shr_full, t)[...] = total
+        total = total + unpack(shr_recv[sender])
+    row_slice(shr_full, t)[...] = pack(total, shr_full.dtype)
 
     def full_copy(k, sender, device):
         return remote(
@@ -303,7 +314,7 @@
         lane = lax.broadcasted_iota(jnp.int32, (q_chunk, HD), 1)
         token_row = pick(pos, token_bounds, adapter_rows, jnp.zeros((q_chunk, HD), jnp.int32))
         half = jnp.where(lane >= HD // 2, 1, 0)
-        shrunk = shr_full[span, :]
+        shrunk = unpack(shr_full[span, :])
         value = base[span, :]
         for s in range(SUB):
             mine = jnp.where(token_row == half + (first + s) * own_adapters, shrunk, 0.0)
@@ -388,9 +399,9 @@
             pltpu.VMEM((SUB, own * rank, width), BF16),
             pltpu.VMEM((n, own, rank, HD), BF16),
             pltpu.VMEM((SUB, tokens, HD), BF16),
-            pltpu.VMEM((tokens, HD), F32),
-            pltpu.VMEM((n, rows, HD), F32),
-            pltpu.VMEM((tokens, HD), F32),
+            pltpu.VMEM((tokens, HD), send_type),
+            pltpu.VMEM((n, rows, HD), send_type),
+            pltpu.VMEM((tokens, HD), send_type),
             pltpu.VMEM((n, rows, width), send_type),
             pltpu.VMEM((n, rows, width), send_type),
             pltpu.VMEM((tokens, width), F32),

time: 93.9 us -> 89.4 us (0.952)
  Pallas kernels: 92 us -> 87.5 us
    pallas_call x1, Pallas kernels: 92 us -> 87.5 us  [on_device(): pl.pallas_call(functools.partial(kernel, n, q_chunk, key_block), out_shap...]
where the time goes in v2:
time: 89.4 us; the launch traced here: 89.2 us
  Pallas kernels  87.5 us (98%)
  local copies, waits for them, and re-layouts  1.72 us (2%)
    pallas_call x1, Pallas kernels, on_device(): pl.pallas_call(functools.partial(kernel, n, q_chunk, key_block), out_shap...  87.5 us

profile of v2, /device:TPU:27, one launch (start us, length us, event | category | flops | bytes accessed | tf_op | source)
XLA Modules:
  0.0 89.2 jit_solution(887501670184201959)
XLA Ops:
  0.0 87.5 %shard_map.118 = bf16[32,5120]{1,0:T(8,128)(2,1)} custom-call(bf16[512,128]{1,0:T(8,128)(2,1)} %q_hbm.1, bf16[512,128]{1,0:T(8,128)(2,1)} %bk_hbm.1, bf16[512,128]{1,0:T(8,128)(2,1)} %bv_hbm.1, bf16[12288,128]{1,0:T(8,128)(2,1)} %ck_hbm.1, bf16[12288,128]{1,0:T(8,128)(2,1)} %cv_hbm.1, bf16[128,5120]{1,0:T(8,128)(2,1)} %w_hbm.1, ...), custom_call_target="tpu_custom_call" | custom-call | tf_op jit(solution)/shard_map/pallas_call | solution.py:389
  87.5 1.7 %copy.14 = bf16[32,5120]{1,0:T(8,128)(2,1)} copy(bf16[32,5120]{1,0:T(8,128)(2,1)} %shard_map.118) | data formatting | bytes 655360

commit v3 on v2

--- a/solution.py
+++ b/solution.py
@@ -67,7 +67,6 @@
     shr_full,
     part,
     recv,
-    base,
     load_sem,
     w_send,
     w_recv,
@@ -83,10 +82,16 @@
     f_recv,
     o_send,
     o_recv,
+    x_send,
+    x_recv,
 ):
     t = lax.axis_index("tensor")
     j = lax.rem(t, SUB)
     first = t - j
+    group = lax.axis_index("groups")
+    shared = lax.axis_size("groups") % 2 == 0
+    side = lax.rem(group, 2)
+    twin = group + 1 - 2 * side
     tokens = q_hbm.shape[0]
     cached = ck_hbm.shape[0]
     requests = block_len.shape[0]
@@ -128,7 +133,14 @@
             device_id={"tensor": lax.rem(t + k, n)},
             device_id_type=pl.DeviceIdType.MESH,
         )
-    pl.semaphore_wait(barrier, n - 1)
+    if shared:
+        pl.semaphore_signal(
+            barrier,
+            inc=1,
+            device_id={"groups": twin, "tensor": t},
+            device_id_type=pl.DeviceIdType.MESH,
+        )
+    pl.semaphore_wait(barrier, n if shared else n - 1)
 
     def remote(src, dst, send_sem, recv_sem, device):
         return pltpu.make_async_remote_copy(
@@ -145,9 +157,27 @@
             s_hbm.at[:, :, heads_columns(device)], s_all.at[sender], s_send.at[k], s_recv.at[k], device
         )
 
+    lines = HD // 2 if shared else HD
+    own_lines = pl.ds(pl.multiple_of(side * lines, lines), lines) if shared else pl.ds(0, HD)
+    twin_lines = pl.ds(pl.multiple_of((1 - side) * lines, lines), lines)
+
     def weight_copy(k, sender_j, jj):
         return remote(
-            w_hbm.at[:, columns(jj)], w_all.at[sender_j], w_send.at[k], w_recv.at[k], first + jj
+            w_hbm.at[own_lines, columns(jj)],
+            w_all.at[sender_j, own_lines],
+            w_send.at[k],
+            w_recv.at[k],
+            first + jj,
+        )
+
+    def twin_copy(k, sender_j, span):
+        return pltpu.make_async_remote_copy(
+            src_ref=w_all.at[sender_j, span],
+            dst_ref=w_all.at[sender_j, span],
+            send_sem=x_send.at[k],
+            recv_sem=x_recv.at[k],
+            device_id={"groups": twin, "tensor": t},
+            device_id_type=pl.DeviceIdType.MESH,
         )
 
     def expand_copy(k, sender_j, jj):
@@ -224,7 +254,7 @@
             device,
         )
 
-    for c in range(chunks):
+    def attend(c):
         q = q2[pl.ds(c * q_chunk, q_chunk), :]
         scores = dot_nt(q, k2[0:tokens, :])
         row = lax.broadcasted_iota(jnp.int32, scores.shape, 0) + c * q_chunk
@@ -243,7 +273,7 @@
             acc = acc * jnp.exp2((top - new_top) * scale)
             return new_top, acc + jnp.dot(p, v2[pl.ds(at, key_block), :], preferred_element_type=F32)
 
-        top, acc = lax.fori_loop(0, cached // key_block, step, (top, acc))
+        top, acc = lax.fori_loop(0, cached // key_block, step, (top, acc), unroll=2)
         attended = (acc[:, :HD] / acc[:, HD:]).astype(BF16)
         span = pl.ds(c * q_chunk, q_chunk)
         att_all[j, span] = attended
@@ -253,6 +283,11 @@
         if c == 0:
             for k in range(1, n):
                 shrink_copy(k, lax.rem(t + n - k, n), t).wait_recv()
+            for k in range(1, SUB):
+                source = lax.rem(j + SUB - k, SUB)
+                weight_copy(k, source, j).wait_recv()
+                if shared:
+                    twin_copy(k, source, own_lines).start()
         pos = lax.broadcasted_iota(jnp.int32, (q_chunk, HD), 0) + c * q_chunk
         lane = lax.broadcasted_iota(jnp.int32, (q_chunk, HD), 1)
         token_row = pick(pos, token_bounds, adapter_rows, jnp.zeros((q_chunk, HD), jnp.int32))
@@ -270,52 +305,57 @@
             def _():
                 shr_copy(t, device).start()
 
-    total = unpack(row_slice(shr_part, t)[...])
-    for k in range(1, n):
-        sender = lax.rem(t + n - k, n)
-        shr_copy_in = remote(
-            row_slice(shr_part, t), shr_recv.at[sender], p_send.at[sender], p_recv.at[sender], sender
-        )
-        shr_copy_in.wait_recv()
-        total = total + unpack(shr_recv[sender])
-    row_slice(shr_full, t)[...] = pack(total, shr_full.dtype)
-
-    def full_copy(k, sender, device):
+    def full_copy(sender, device):
         return remote(
-            row_slice(shr_full, sender), row_slice(shr_full, sender), f_send.at[k], f_recv.at[k], device
-        )
-
-    for k in range(1, n):
-        full_copy(k, t, lax.rem(t + k, n)).start()
-
-    for k in range(1, SUB):
-        source = lax.rem(j + SUB - k, SUB)
-        weight_copy(k, source, j).wait_recv()
-        for c in range(chunks):
+            row_slice(shr_full, sender),
+            row_slice(shr_full, sender),
+            f_send.at[device],
+            f_recv.at[sender],
+            device,
+        )
+
+    def collect(c):
+        @pl.when(t // per_chunk == c)
+        def _():
+            total = unpack(row_slice(shr_part, t)[...])
+            for k in range(1, n):
+                sender = lax.rem(t + n - k, n)
+                shr_copy_in = remote(
+                    row_slice(shr_part, t), shr_recv.at[sender], p_send.at[sender], p_recv.at[sender], sender
+                )
+                shr_copy_in.wait_recv()
+                total = total + unpack(shr_recv[sender])
+            row_slice(shr_full, t)[...] = pack(total, shr_full.dtype)
+            for k in range(1, n):
+                full_copy(t, lax.rem(t + k, n)).start()
+
+    def part_copy(sender, device):
+        return remote(part.at[device], recv.at[sender], o_send.at[device], o_recv.at[sender], device)
+
+    def project(c):
+        for k in range(1, SUB):
+            source = lax.rem(j + SUB - k, SUB)
             att_copy(c, k, source, j).wait_recv()
-    for c in range(chunks):
+            if c == 0:
+                if shared:
+                    twin_copy(k, source, twin_lines).wait_recv()
+                expand_copy(k, source, j).wait_recv()
+        for k in range(per_chunk):
+            owner = c * per_chunk + lax.rem(t + k, per_chunk)
+
+            @pl.when(owner != t)
+            def _():
+                full_copy(owner, t).wait_recv()
+
         span = pl.ds(c * q_chunk, q_chunk)
         value = jnp.dot(att_all[0, span], w_all[0], preferred_element_type=F32)
         for s in range(1, SUB):
             value = value + jnp.dot(att_all[s, span], w_all[s], preferred_element_type=F32)
-        base[span, :] = value
-
-    for k in range(1, SUB):
-        expand_copy(k, lax.rem(j + SUB - k, SUB), j).wait_recv()
-    for k in range(1, n):
-        full_copy(k, lax.rem(t + n - k, n), t).wait_recv()
-
-    def part_copy(sender, device):
-        return remote(part.at[device], recv.at[sender], o_send.at[device], o_recv.at[sender], device)
-
-    for c in range(chunks):
-        span = pl.ds(c * q_chunk, q_chunk)
         pos = lax.broadcasted_iota(jnp.int32, (q_chunk, HD), 0) + c * q_chunk
         lane = lax.broadcasted_iota(jnp.int32, (q_chunk, HD), 1)
         token_row = pick(pos, token_bounds, adapter_rows, jnp.zeros((q_chunk, HD), jnp.int32))
         half = jnp.where(lane >= HD // 2, 1, 0)
         shrunk = unpack(shr_full[span, :])
-        value = base[span, :]
         for s in range(SUB):
             mine = jnp.where(token_row == half + (first + s) * own_adapters, shrunk, 0.0)
             high = mine.astype(BF16)
@@ -331,6 +371,15 @@
             def _():
                 part_copy(t, device).start()
 
+    for c in range(chunks):
+        attend(c)
+        if c > 0:
+            collect(c - 1)
+    project(0)
+    collect(chunks - 1)
+    for c in range(1, chunks):
+        project(c)
+
     recv[t] = part[t]
     for k in range(1, n):
         sender = lax.rem(t + n - k, n)
@@ -345,12 +394,14 @@
     for k in range(1, n):
         device = lax.rem(t + k, n)
         shrink_copy(k, t, device).wait_send()
-        full_copy(k, t, device).wait_send()
+        full_copy(t, device).wait_send()
         shr_copy(t, device).wait_send()
         part_copy(t, device).wait_send()
     for k in range(1, SUB):
         jj = lax.rem(j + k, SUB)
         weight_copy(k, j, jj).wait_send()
+        if shared:
+            twin_copy(k, jj, own_lines).wait_send()
         expand_copy(k, j, jj).wait_send()
         for c in range(chunks):
             att_copy(c, k, j, jj).wait_send()
@@ -377,8 +428,8 @@
     own, _, rank = stored_shrink_matrices.shape
     rows = tokens // n
     width = model // SUB
-    q_chunk = 256
-    key_block = 1536
+    q_chunk = 128
+    key_block = 3072
     chunks = tokens // q_chunk
     send_type = BF16 if rows % 16 == 0 else F32
     shrink_t = stored_shrink_matrices.transpose(0, 2, 1)
@@ -404,7 +455,6 @@
             pltpu.VMEM((tokens, HD), send_type),
             pltpu.VMEM((n, rows, width), send_type),
             pltpu.VMEM((n, rows, width), send_type),
-            pltpu.VMEM((tokens, width), F32),
             dma((8,)),
             dma((SUB,)),
             dma((SUB,)),
@@ -420,6 +470,8 @@
             dma((n,)),
             dma((n,)),
             dma((n,)),
+            dma((SUB,)),
+            dma((SUB,)),
         ],
         compiler_params=pltpu.CompilerParams(
             collective_id=0, has_side_effects=True, vmem_limit_bytes=56 * 1024 * 1024

time: 89.4 us -> 82.9 us (0.927)
  Pallas kernels: 87.5 us -> 81 us
    pallas_call x1, Pallas kernels: 87.5 us -> 81 us  [on_device(): pl.pallas_call(functools.partial(kernel, n, q_chunk, key_block), out_shap...]
where the time goes in v3:
time: 82.9 us; the launch traced here: 82.8 us
  Pallas kernels  81 us (98%)
  local copies, waits for them, and re-layouts  1.72 us (2%)
    pallas_call x1, Pallas kernels, on_device(): pl.pallas_call(functools.partial(kernel, n, q_chunk, key_block), out_shap...  81 us
    unnamed x1, local copies, waits for them, and re-layouts  1.72 us

profile of v3, /device:TPU:27, one launch (start us, length us, event | category | flops | bytes accessed | tf_op | source)
XLA Modules:
  0.0 82.8 jit_solution(1728860381879458365)
XLA Ops:
  0.0 81.0 %shard_map.118 = bf16[32,5120]{1,0:T(8,128)(2,1)} custom-call(bf16[512,128]{1,0:T(8,128)(2,1)} %q_hbm.1, bf16[512,128]{1,0:T(8,128)(2,1)} %bk_hbm.1, bf16[512,128]{1,0:T(8,128)(2,1)} %bv_hbm.1, bf16[12288,128]{1,0:T(8,128)(2,1)} %ck_hbm.1, bf16[12288,128]{1,0:T(8,128)(2,1)} %cv_hbm.1, bf16[128,5120]{1,0:T(8,128)(2,1)} %w_hbm.1, ...), custom_call_target="tpu_custom_call" | custom-call | tf_op jit(solution)/shard_map/pallas_call | solution.py:440
  81.0 1.7 %copy.14 = bf16[32,5120]{1,0:T(8,128)(2,1)} copy(bf16[32,5120]{1,0:T(8,128)(2,1)} %shard_map.118) | data formatting | bytes 655360
